TPU v7x, 32 devices: a whole 2x2x4 slice. The times are simulated.
32 devices in a mesh: rows: 8 (over z, x), seq: 4 (over y, core).
Axes of the slice: x: 2, y: 2, z: 4, core: 2. Of those that a mesh axis runs over, the one named last changes fastest.
Arguments:
- frames_in: bfloat16 [16, 4096, 512], P('rows', 'seq'), may hold values from -6 to 6
- lengths: int32 [16, 4], P('rows'), may hold values from 1 to 2048, 4096 in all within a row
- bw_ids: int32 [16, 4], P('rows'), may hold values from 0 to 3
- owner_list: int32 [137], replicated, may hold values from 0 to 7, as said below
- master: float32 [216, 32, 512], P('rows')
- moment1: float32 [216, 32, 512], P('rows')
- moment2: float32 [216, 32, 512], P('rows'), as said below
- wave_grad: bfloat16 [16, 1310720], P('rows', 'seq'), may hold values from -6 to 6
Outputs:
- waveform: float32 [16, 1310720], P('rows', 'seq')
- input_grad: float32 [16, 4096, 512], P('rows', 'seq')
- new_master: float32 [216, 32, 512], P('rows')
- new_moment1: float32 [216, 32, 512], P('rows')
- new_moment2: float32 [216, 32, 512], P('rows')
Inputs may be any that keep to these rules, and one draw needn't show every extreme that they name: `owner_list`: no index along rows owns more than 27 buckets, and some index owns exactly 27. `moment2`: every entry is positive.
All inputs are finite; a program needn't handle non-finite values.
Results may differ from a plain program's by a relative error of at most 0.012.
The roundings to bfloat16 on the way count: a program that leaves them out, or rounds other values in their place, can miss the bound.
Values may be sent and summed in bfloat16 or wider, within the bound.
No kernel may reach another device: no remote copies, remote signals or barrier semaphores. Data moves between devices by JAX's collectives and lax.ppermute only.
A program may use at most 192 MiB of HBM per device.

v0:
```python
import math
import jax
import jax.numpy as jnp
from jax import lax
from jax.sharding import PartitionSpec as P

FF = 1536
NFFT = 1280
HOP = 320
NBW = 4
KW = 7
UTT = 4
BR = 32
STEP_COUNT = 6
BINS = 641
NOUT = 1282
VROWS = 20
IN_ROWS = 3
HEAD_ROWS = 3
PR = 4380
NB = 137
NORM_EPS = 1e-06
ENV_FLOOR = 0.5
BETA_ONE = 0.8
BETA_TWO = 0.9
LEARN_RATE = 0.04
WEIGHT_DECAY = 0.01
ADAM_EPS = 1e-08


def padded(block, sides, width):
    for axis, dim in sides:
        count = lax.axis_size(axis)
        forward = [(i, i + 1) for i in range(count - 1)]
        backward = [(target, source) for source, target in forward]
        low = lax.ppermute(
            lax.slice_in_dim(block, block.shape[dim] - width, None, axis=dim), axis, forward
        )
        high = lax.ppermute(lax.slice_in_dim(block, 0, width, axis=dim), axis, backward)
        block = jnp.concatenate([low, block, high], axis=dim)
    return block


def from_behind(block, axis, distance):
    devices = range(lax.axis_size(axis))
    route = [(i - distance, i) for i in devices if i - distance in devices]
    return lax.ppermute(block, axis, route)


def slot_maps(owner_list, owner_count, slot_count):
    bucket_count = owner_list.shape[0]
    bucket_index = jnp.arange(bucket_count, dtype=jnp.int32)
    same_owner = owner_list[None, :] == owner_list[:, None]
    before = bucket_index[None, :] < bucket_index[:, None]
    slot_rank = jnp.sum((same_owner & before).astype(jnp.int32), axis=1)
    bucket_place = owner_list * slot_count + slot_rank
    targets = jnp.arange(owner_count * slot_count, dtype=jnp.int32)
    slot_match = bucket_place[None, :] == targets[:, None]
    found_bucket = jnp.sum(slot_match.astype(jnp.int32) * bucket_index[None, :], axis=1)
    source = jnp.where(jnp.any(slot_match, axis=1), found_bucket, bucket_count)
    return (bucket_place, source)


def synthesis_table():
    bin_index = jnp.arange(BINS, dtype=jnp.int32)[:, None]
    tap_index = jnp.arange(NFFT, dtype=jnp.int32)[None, :]
    turns = bin_index * tap_index % NFFT
    angle = turns.astype(jnp.float32) * (2.0 * math.pi / NFFT)
    edge_bin = (bin_index == 0) | (bin_index == NFFT // 2)
    factor = jnp.where(edge_bin, 1.0, 2.0).astype(jnp.float32) / NFFT
    return jnp.concatenate([factor * jnp.cos(angle), -factor * jnp.sin(angle)], axis=0)


def hann_window():
    angle = jnp.arange(NFFT, dtype=jnp.int32).astype(jnp.float32) * (2.0 * math.pi / NFFT)
    return 0.5 - 0.5 * jnp.cos(angle)


def segment_ids(lengths, first_index, span):
    starts = jnp.cumsum(lengths, axis=1) - lengths
    frame_index = first_index + jnp.arange(span, dtype=jnp.int32)
    return jnp.sum((starts[:, None, :] <= frame_index[None, :, None]).astype(jnp.int32), axis=2) - 1


def layer_norm(values):
    row_mean = jnp.mean(values, axis=-1, keepdims=True)
    centered = values - row_mean
    return centered * lax.rsqrt(jnp.mean(centered * centered, axis=-1, keepdims=True) + NORM_EPS)


def ada_norm(values, scale_rows, shift_rows):
    return layer_norm(values) * scale_rows + shift_rows


def final_norm(values, norm_gain, norm_bias):
    return layer_norm(values) * norm_gain[None, :] + norm_bias[None, :]


def exact_gelu(values):
    return jax.nn.gelu(values, approximate=False)


def contract(left_side, right_side, left_dim, right_dim):
    return lax.dot_general(
        left_side,
        right_side,
        (((left_dim,), (right_dim,)), ((), ())),
        preferred_element_type=jnp.float32,
    )


def local(frames_in, lengths, bw_ids, owner_list, master, moment1, moment2, wave_grad):
    rows_here, frames_here, channels = frames_in.shape
    slot_count = master.shape[0]
    frame_count = rows_here * frames_here
    lap_count = NFFT // HOP
    rim_width = (KW - 1) // 2
    margin = max(rim_width, lap_count - 1)
    bucket_place, source = slot_maps(owner_list, lax.axis_size("rows"), slot_count)
    gathered = lax.all_gather(master.astype(jnp.bfloat16), "rows", axis=0, tiled=True)
    buckets = jnp.take(gathered, bucket_place, axis=0)
    weight_table = buckets.reshape(-1, channels)[:PR]
    w_in = weight_table[:FF]
    w_out = weight_table[FF : 2 * FF]
    w_head = weight_table[2 * FF : 2 * FF + NOUT]
    row_start = 2 * FF + NOUT
    channel_rows = weight_table[row_start : row_start + VROWS].astype(jnp.float32)
    row_start = row_start + VROWS
    bias_in = weight_table[row_start : row_start + IN_ROWS].reshape(-1).astype(jnp.float32)
    row_start = row_start + IN_ROWS
    bias_head = (
        weight_table[row_start : row_start + HEAD_ROWS].reshape(-1)[:NOUT].astype(jnp.float32)
    )
    conv_weight = channel_rows[:KW]
    conv_bias = channel_rows[KW]
    ada_scale = channel_rows[KW + 1 : KW + 1 + NBW]
    ada_shift = channel_rows[KW + 1 + NBW : KW + 1 + 2 * NBW]
    vec_base = KW + 1 + 2 * NBW
    bias_out = channel_rows[vec_base]
    layer_scale = channel_rows[vec_base + 1]
    norm_gain = channel_rows[vec_base + 2]
    norm_bias = channel_rows[vec_base + 3]
    first_index = lax.axis_index("seq") * frames_here - margin
    segment = segment_ids(lengths, first_index, frames_here + 2 * margin)
    own_segment = segment[:, margin : margin + frames_here]
    halo_frames = padded(frames_in, (("seq", 1),), rim_width)
    wide_frames = halo_frames.astype(jnp.float32)
    conv_keep = []
    conv_out = jnp.zeros((rows_here, frames_here, channels), jnp.float32) + conv_bias
    for tap_index in range(KW):
        lower = margin - rim_width + tap_index
        keep = (segment[:, lower : lower + frames_here] == own_segment).astype(jnp.float32)[
            :, :, None
        ]
        conv_keep.append(keep)
        conv_out = (
            conv_out
            + keep * wide_frames[:, tap_index : tap_index + frames_here] * conv_weight[tap_index]
        )
    conv_out = conv_out.reshape(frame_count, channels)
    utt_pick = (own_segment[:, :, None] == jnp.arange(UTT, dtype=jnp.int32)[None, None, :]).astype(
        jnp.int32
    )
    frame_ids = jnp.sum(utt_pick * bw_ids[:, None, :], axis=2).reshape(frame_count)
    bw_onehot = (frame_ids[:, None] == jnp.arange(NBW, dtype=jnp.int32)[None, :]).astype(
        jnp.float32
    )
    scale_rows = jnp.dot(bw_onehot, ada_scale, precision=lax.Precision.HIGHEST)
    shift_rows = jnp.dot(bw_onehot, ada_shift, precision=lax.Precision.HIGHEST)
    ada_value, ada_back = jax.vjp(ada_norm, conv_out, scale_rows, shift_rows)
    ada_low = ada_value.astype(jnp.bfloat16)
    hidden_pre = contract(ada_low, w_in, 1, 1) + bias_in[None, :]
    act_value, gelu_back = jax.vjp(exact_gelu, hidden_pre)
    act_low = act_value.astype(jnp.bfloat16)
    branch = contract(act_low, w_out, 1, 0) + bias_out[None, :]
    frames_flat = frames_in.reshape(frame_count, channels).astype(jnp.float32)
    residual = frames_flat + layer_scale[None, :] * branch
    normed_value, final_back = jax.vjp(final_norm, residual, norm_gain, norm_bias)
    normed_low = normed_value.astype(jnp.bfloat16)
    head_out = contract(normed_low, w_head, 1, 1) + bias_head[None, :]
    magnitude = jnp.exp(head_out[:, :BINS])
    phase_angle = head_out[:, BINS:]
    real_part = magnitude * jnp.cos(phase_angle)
    imag_part = magnitude * jnp.sin(phase_angle)
    spectrum_low = jnp.concatenate([real_part, imag_part], axis=1).astype(jnp.bfloat16)
    synthesis = synthesis_table().astype(jnp.bfloat16)
    signal = contract(spectrum_low, synthesis, 1, 0)
    window_rows = hann_window().reshape(lap_count, HOP)
    pieces = signal.reshape(rows_here, frames_here, lap_count, HOP) * window_rows[None, None, :, :]
    lap_keep = []
    numerator = jnp.zeros((rows_here, frames_here + lap_count - 1, HOP), jnp.float32)
    envelope = jnp.zeros((rows_here, frames_here, HOP), jnp.float32)
    for lap_index in range(lap_count):
        ahead = margin + lap_index
        keep = (segment[:, ahead : ahead + frames_here] == own_segment).astype(jnp.float32)[
            :, :, None
        ]
        lap_keep.append(keep)
        numerator = numerator + jnp.pad(
            keep * pieces[:, :, lap_index], ((0, 0), (lap_index, lap_count - 1 - lap_index), (0, 0))
        )
        behind = margin - lap_index
        back_keep = (segment[:, behind : behind + frames_here] == own_segment).astype(jnp.float32)[
            :, :, None
        ]
        envelope = envelope + back_keep * (window_rows[lap_index] ** 2)[None, None, :]
    arrived = from_behind(numerator[:, frames_here:], "seq", 1)
    numerator = numerator[:, :frames_here] + jnp.pad(
        arrived, ((0, 0), (0, frames_here - lap_count + 1), (0, 0))
    )
    denominator = jnp.maximum(envelope, ENV_FLOOR)
    waveform = (numerator / denominator).reshape(rows_here, frames_here * HOP)
    scaled = wave_grad.astype(jnp.float32).reshape(rows_here, frames_here, HOP) / denominator
    later_rows = from_behind(scaled[:, : lap_count - 1], "seq", -1)
    reach_rows = jnp.concatenate([scaled, later_rows], axis=1)
    signal_grad = jnp.stack(
        [
            lap_keep[lap_index]
            * window_rows[lap_index][None, None, :]
            * reach_rows[:, lap_index : lap_index + frames_here]
            for lap_index in range(lap_count)
        ],
        axis=2,
    )
    signal_low = signal_grad.reshape(frame_count, NFFT).astype(jnp.bfloat16)
    spec_grad = contract(signal_low, synthesis, 1, 1)
    real_grad = spec_grad[:, :BINS]
    imag_grad = spec_grad[:, BINS:]
    head_grad = jnp.concatenate(
        [
            real_grad * real_part + imag_grad * imag_part,
            imag_grad * real_part - real_grad * imag_part,
        ],
        axis=1,
    ).astype(jnp.bfloat16)
    grad_w_head = contract(head_grad, normed_low, 0, 0)
    grad_b_head = jnp.sum(head_grad, axis=0, dtype=jnp.float32)
    normed_grad = contract(head_grad, w_head, 1, 0)
    residual_grad, grad_gain, grad_bias = final_back(normed_grad)
    branch_low = (layer_scale[None, :] * residual_grad).astype(jnp.bfloat16)
    grad_layer_scale = jnp.sum(residual_grad * branch, axis=0)
    grad_w_out = contract(act_low, branch_low, 0, 0)
    grad_b_out = jnp.sum(branch_low, axis=0, dtype=jnp.float32)
    act_grad = contract(branch_low, w_out, 1, 1)
    pre_low = gelu_back(act_grad)[0].astype(jnp.bfloat16)
    grad_w_in = contract(pre_low, ada_low, 0, 0)
    grad_b_in = jnp.sum(pre_low, axis=0, dtype=jnp.float32)
    ada_grad = contract(pre_low, w_in, 1, 0)
    conv_grad, scale_grad_rows, shift_grad_rows = ada_back(ada_grad)
    grad_scales = lax.dot_general(
        bw_onehot, scale_grad_rows, (((0,), (0,)), ((), ())), precision=lax.Precision.HIGHEST
    )
    grad_shifts = lax.dot_general(
        bw_onehot, shift_grad_rows, (((0,), (0,)), ((), ())), precision=lax.Precision.HIGHEST
    )
    conv_rows = conv_grad.reshape(rows_here, frames_here, channels)
    grad_conv_b = jnp.sum(conv_grad, axis=0)
    grad_conv_w = jnp.stack(
        [
            jnp.sum(
                conv_keep[tap_index]
                * conv_rows
                * wide_frames[:, tap_index : tap_index + frames_here],
                axis=(0, 1),
            )
            for tap_index in range(KW)
        ],
        axis=0,
    )
    halo_grad = padded(conv_rows, (("seq", 1),), rim_width)
    input_grad = residual_grad.reshape(rows_here, frames_here, channels)
    for tap_index in range(KW):
        lower = margin + rim_width - tap_index
        keep = (segment[:, lower : lower + frames_here] == own_segment).astype(jnp.float32)[
            :, :, None
        ]
        begin = 2 * rim_width - tap_index
        input_grad = (
            input_grad + conv_weight[tap_index] * keep * halo_grad[:, begin : begin + frames_here]
        )
    vec_grads = jnp.concatenate(
        [
            grad_conv_w,
            grad_conv_b[None, :],
            grad_scales,
            grad_shifts,
            jnp.stack([grad_b_out, grad_layer_scale, grad_gain, grad_bias], axis=0),
        ],
        axis=0,
    )
    in_rows = grad_b_in.reshape(IN_ROWS, channels)
    head_rows = jnp.pad(grad_b_head, (0, HEAD_ROWS * channels - NOUT)).reshape(HEAD_ROWS, channels)
    grad_table = jnp.concatenate(
        [grad_w_in, grad_w_out, grad_w_head, vec_grads, in_rows, head_rows], axis=0
    )
    grad_buckets = jnp.pad(grad_table, ((0, NB * BR - PR), (0, 0))).reshape(NB, BR, channels)
    empty_bucket = jnp.zeros((1, BR, channels), jnp.float32)
    summed = lax.psum(grad_buckets, ("rows", "seq"))
    extended = jnp.concatenate([summed, empty_bucket], axis=0)
    my_sources = lax.dynamic_slice_in_dim(source, lax.axis_index("rows") * slot_count, slot_count)
    reduced = jnp.take(extended, my_sources, axis=0)
    first_new = BETA_ONE * moment1 + (1.0 - BETA_ONE) * reduced
    second_new = BETA_TWO * moment2 + (1.0 - BETA_TWO) * reduced * reduced
    first_fix = 1.0 - BETA_ONE**STEP_COUNT
    second_fix = 1.0 - BETA_TWO**STEP_COUNT
    master_new = master - LEARN_RATE * (
        first_new / first_fix / (jnp.sqrt(second_new / second_fix) + ADAM_EPS)
        + WEIGHT_DECAY * master
    )
    return (waveform, input_grad, master_new, first_new, second_new)


def solution(mesh):
    in_specs = (
        P("rows", "seq", None),
        P("rows", None),
        P("rows", None),
        P(),
        P("rows", None, None),
        P("rows", None, None),
        P("rows", None, None),
        P("rows", "seq"),
    )
    out_specs = (
        P("rows", "seq"),
        P("rows", "seq", None),
        P("rows", None, None),
        P("rows", None, None),
        P("rows", None, None),
    )
    return jax.shard_map(local, mesh=mesh, in_specs=in_specs, out_specs=out_specs, check_vma=False)
```

profile of v0, /device:TPU:0, one launch (start us, length us, event | category | flops | bytes accessed | tf_op | source)
XLA Modules:
  0.0 546.3 jit_solution(15566940357598605938)
XLA Ops:
  35.9 15.2 %multiply_convert_fusion.2 = (bf16[641,1280]{1,0:T(8,128)(2,1)}, bf16[641,1280]{1,0:T(8,128)(2,1)}) fusion(f32[641]{0:T(1024)S(1)} %fusion.74, f32[641]{0:T(1024)S(1)} %select_multiply_fusion), kind=kLoop, calls=%fused_computation.89 | loop fusion | flops 10666240 | bytes 3287048 | tf_op jit(solution)/shard_map/convert.12
  51.9 9.4 %concatenate.35 = bf16[2,1030,512]{2,1,0:T(8,128)(2,1)S(1)} concatenate(bf16[2,3,512]{2,1,0:T(4,128)(2,1)S(1)} %collective-permute-done, bf16[2,1024,512]{2,1,0:T(8,128)(2,1)} %param.8, bf16[2,3,512]{2,1,0:T(4,128)(2,1)S(1)} %collective-permute-done.1), dimensions={1} | concatenate | bytes 4218880 | tf_op jit(solution)/shard_map/concatenate | solution.py:40
  63.8 4.7 fusion.55
  71.7 10.2 %copy.40 = bf16[2,1024,4,320]{1,0,3,2:T(2,128)(2,1)} copy(bf16[2,1024,4,320]{1,3,0,2:T(8,128)(2,1)} %pad_maximum_fusion.1) | data formatting | bytes 10485760 | tf_op jit(solution)/shard_map/stack | solution.py:216
  81.9 4.8 copy.45
  86.7 9.7 %fusion.49 = f32[2048,1282]{0,1:T(8,128)} fusion(bf16[2048,1280]{0,1:T(8,128)(2,1)S(1)} %bitcast.122, bf16[641,1280]{1,0:T(8,128)(2,1)S(1)} %copy-done.20, bf16[641,1280]{1,0:T(8,128)(2,1)S(1)} %copy-done.21), kind=kOutput, calls=%fused_computation.122 | convolution fusion | flops 6727936000 | bytes 19026944 | tf_op jit(solution)/shard_map/dot_general | solution.py:104
  96.5 25.9 %all-gather.2.cloned.1.call-done = bf16[216,32,512]{2,1,0:T(8,128)(2,1)} async-done(((bf16[27,32,512]{2,1,0:T(8,128)(2,1)}), bf16[216,32,512]{2,1,0:T(8,128)(2,1)}) %all-gather.2.cloned.1.call-update) | async-done | bytes 7077904 | tf_op jit(solution)/shard_map/all_gather | solution.py:120
  122.3 10.9 %gather_fusion = bf16[137,32,512]{2,1,0:T(8,128)(2,1)} fusion(bf16[216,32,512]{2,1,0:T(8,128)(2,1)} %all-gather.2.cloned.1.call-done, s32[1024]{0:T(1024)S(1)} %pad_clamp_fusion.1), kind=kCustom, calls=%fused_computation | custom fusion | bytes 8978980 | tf_op jit(solution)/shard_map/jit(_take)/gather | solution.py:121
  133.3 4.1 bitcast_select_fusion
  142.7 6.1 %fusion.88 = (f32[2,1024]{1,0:T(2,128)S(1)}, f32[2,1024,512]{2,1,0:T(8,128)S(1)}) fusion(f32[512]{0:T(512)S(1)} %bitcast.134, f32[2,1030,512]{2,1,0:T(8,128)S(1)} %bitcast.114, f32[2,1024]{1,0:T(2,128)S(1)} %get-tuple-element.69, f32[512]{0:T(512)S(1)} %bitcast.136, f32[2,1024]{1,0:T(2,128)S(1)} %get-tuple-element.70, f32[512]{0:T(512)S(1)} %bitcast.138, ...), kind=kLoop, calls=%fused_computation.211 | loop fusion | flops 22018048 | bytes 33628160 | tf_op jit(solution)/shard_map/jvp()/reduce_sum | solution.py:86
  161.8 31.4 %multiply_convert_fusion = (bf16[2048,1536]{1,0:T(8,128)(2,1)S(1)}, f32[2048,1536]{1,0:T(8,128)}, f32[2048,1536]{1,0:T(8,128)}) fusion(f32[1536]{0:T(1024)S(1)} %reshape.280, bf16[2048,512]{1,0:T(8,128)(2,1)S(1)} %add_convert_fusion.3, bf16[1536,512]{1,0:T(8,128)(2,1)S(1)} %bitcast.123), kind=kOutput, calls=%fused_computation.6 | convolution fusion | flops 3428843520 | bytes 35133440 | tf_op jit(solution)/shard_map/dot_general | solution.py:104
  193.2 5.6 %fusion.86 = (f32[2048]{0:T(1024)S(1)}, f32[2048,512]{1,0:T(8,128)S(1)}, f32[2048,512]{1,0:T(8,128)}) fusion(f32[512]{0:T(512)S(1)} %bitcast.159, f32[512]{0:T(512)S(1)} %bitcast.157, bf16[2,1024,512]{2,1,0:T(8,128)(2,1)S(1)} %copy-done.16, bf16[2048,1536]{1,0:T(8,128)(2,1)S(1)} %get-tuple-element.32, bf16[1536,512]{1,0:T(8,128)(2,1)S(1)} %bitcast.125), kind=kOutput, calls=%fused_computation.210 | convolution fusion | flops 3226466304 | bytes 18362368 | tf_op jit(solution)/shard_map/dot_general | solution.py:104
  201.6 5.8 %convolution_add_fusion = f32[2048,1282]{0,1:T(8,128)S(1)} fusion(f32[1282]{0:T(1024)S(1)} %slice_convert_fusion.1, bf16[4384,512]{1,0:T(8,128)(2,1)} %copy-done.13, f32[2048,512]{1,0:T(8,128)} %copy-done.8, f32[512]{0:T(512)S(1)} %bitcast.169, f32[512]{0:T(512)S(1)} %bitcast.163, f32[2048]{0:T(1024)S(1)} %fusion.70, f32[2048]{0:T(1024)S(1)} %broadcast_multiply_fusion), kind=kOutput, calls=%fused_computation.22 | convolution fusion | flops 2696417280 | bytes 16040968 | tf_op jit(solution)/shard_map/dot_general | solution.py:104
  207.5 24.2 %add_convert_fusion.1 = (bf16[2048,641]{0,1:T(8,128)(2,1)S(1)}, bf16[2048,641]{0,1:T(8,128)(2,1)S(1)}, bf16[2048,641]{0,1:T(8,128)(2,1)}, bf16[2048,641]{0,1:T(8,128)(2,1)}) fusion(f32[2048,1282]{0,1:T(8,128)} %fusion.49, f32[2048,1282]{0,1:T(8,128)S(1)} %convolution_add_fusion), kind=kLoop, calls=%fused_computation.31 | loop fusion | flops 15753216 | bytes 31506432 | tf_op jit(solution)/shard_map/convert.2
  233.9 6.2 %multiply_reduce_fusion = (f32[512]{0:T(512)S(1)}, f32[2048]{0:T(1024)S(1)}, f32[512]{0:T(512)S(1)}, f32[2048,512]{1,0:T(8,128)S(1)}) fusion(f32[2048,512]{1,0:T(8,128)S(1)} %copy-done.9, f32[2048]{0:T(1024)S(1)} %fusion.70, f32[2048]{0:T(1024)S(1)} %broadcast_multiply_fusion, f32[512]{0:T(512)S(1)} %bitcast.164, bf16[4384,512]{1,0:T(8,128)(2,1)} %copy-done.13, ...), kind=kOutput, calls=%fused_computation.64 | convolution fusion | flops 2707436544 | bytes 14989312 | tf_op jit(solution)/shard_map/dot_general | solution.py:104
  240.1 4.6 fusion.52
  253.1 16.6 %convert_reduce_fusion = (f32[1536]{0:T(1024)S(1)}, bf16[2048,1536]{1,0:T(8,128)(2,1)}) fusion(f32[2048,1536]{1,0:T(8,128)} %get-tuple-element.33, bf16[2048,512]{1,0:T(8,128)(2,1)} %copy-done.19, bf16[1536,512]{1,0:T(8,128)(2,1)} %bitcast.126, f32[2048,1536]{1,0:T(8,128)} %get-tuple-element.84, f32[1536]{0:T(1024)S(1)} %reshape.280), kind=kOutput, calls=%fused_computation.4 | convolution fusion | flops 3274701312 | bytes 35139584 | tf_op jit(solution)/shard_map/dot_general | solution.py:104
  269.7 6.7 %multiply_reduce_fusion.9 = (f32[2048]{0:T(1024)S(1)}, f32[2048,512]{1,0:T(8,128)S(1)}) fusion(f32[2048,512]{1,0:T(8,128)S(1)} %copy-done.4, f32[2048,512]{1,0:T(8,128)S(1)} %copy-done.6, bf16[2048,1536]{1,0:T(8,128)(2,1)} %get-tuple-element.90, bf16[1536,512]{1,0:T(8,128)(2,1)} %bitcast.124), kind=kOutput, calls=%fused_computation.76 | convolution fusion | flops 3224369152 | bytes 20455424 | tf_op jit(solution)/shard_map/dot_general | solution.py:104
  276.4 5.1 fusion.94
  285.5 5.5 %fusion.84 = (f32[2048]{0:T(1024)S(1)}, f32[2048,512]{1,0:T(8,128)S(1)}) fusion(f32[2048]{0:T(1024)S(1)} %fusion.69, f32[2048]{0:T(1024)S(1)} %copy-done.39, f32[2048,512]{1,0:T(8,128)} %copy-done.7, f32[2048,512]{1,0:T(8,128)} %fusion.60, f32[2048]{0:T(1024)S(1)} %bitcast.132, f32[2,1024,512]{2,1,0:T(8,128)} %copy-done), kind=kLoop, calls=%fused_computation.208 | loop fusion | flops 7337984 | bytes 16809984 | tf_op jit(solution)/shard_map/transpose(jvp())/reduce_sum | solution.py:87
  294.7 5.3 multiply_reduce_fusion.2
  300.1 27.2 %concatenate.42 = f32[4380,512]{1,0:T(8,128)} concatenate(f32[1536,512]{1,0:T(8,128)} %fusion.94, f32[1536,512]{1,0:T(8,128)S(1)} %fusion.95, f32[1282,512]{1,0:T(8,128)} %fusion.52, f32[1,512]{1,0:T(1,128)S(1)} %bitcast.156, f32[1,512]{1,0:T(1,128)S(1)} %bitcast.155, f32[1,512]{1,0:T(1,128)S(1)} %bitcast.154, f32[1,512]{1,0:T(1,128)S(1)} %bitcast.153, f32[1,512]{1,0:T(1,128)S(1)} %bitcast.152, ...), dimensions={0} | concatenate | bytes 17940480 | tf_op jit(solution)/shard_map/concatenate | solution.py:293
  327.2 8.1 %pad.35 = f32[4384,512]{1,0:T(8,128)} pad(f32[4380,512]{1,0:T(8,128)} %concatenate.42, f32[]{:T(128)} %constant.72.clone.1), padding=0_4x0_0 | pad | bytes 17948676 | tf_op jit(solution)/shard_map/jit(_pad)/pad | solution.py:296
  337.1 13.9 %fusion.6 = f32[2048,1280]{0,1:T(8,128)} fusion(bf16[2048,641]{0,1:T(8,128)(2,1)} %get-tuple-element.41, bf16[2048,641]{0,1:T(8,128)(2,1)S(1)} %copy-done.15, bf16[641,1280]{1,0:T(8,128)(2,1)} %get-tuple-element.91, bf16[641,1280]{1,0:T(8,128)(2,1)} %get-tuple-element.92), kind=kOutput, calls=%fused_computation.34 | convolution fusion | flops 6738438144 | bytes 19018752 | tf_op jit(solution)/shard_map/dot_general | solution.py:104
  350.9 14.4 %reshape.268 = f32[2,1024,4,320]{1,0,3,2:T(2,128)} reshape(f32[2048,1280]{0,1:T(8,128)} %fusion.6) | data formatting | bytes 20971520 | tf_op jit(solution)/shard_map/reshape | solution.py:189
  365.4 8.5 %copy_multiply_fusion = f32[2,1024,4,320]{1,3,0,2:T(8,128)S(1)} fusion(f32[2,1024,4,320]{1,0,3,2:T(2,128)} %reshape.268, f32[4,320]{1,0:T(4,128)S(1)} %copy-done.52), kind=kLoop, calls=%fused_computation.21 | loop fusion | flops 2621440 | bytes 20976640 | tf_op jit(solution)/shard_map/mul | solution.py:189
  382.3 4.4 collective-permute-start.5
  396.1 20.3 %fusion.13 = f32[2,1024,512]{2,1,0:T(8,128)} fusion(f32[2,3,512]{2,1,0:T(4,128)S(1)} %collective-permute-done.5, f32[2,3,512]{2,1,0:T(4,128)S(1)} %collective-permute-done.4, f32[2,1024,512]{2,1,0:T(8,128)} %bitcast.119, f32[2,1024,512]{2,1,0:T(8,128)} %bitcast.118, f32[512]{0:T(512)S(1)} %bitcast.135, f32[2,1024]{1,0:T(2,128)S(1)} %copy-done.31, ...), kind=kLoop, calls=%fused_computation.46 | loop fusion | flops 27262976 | bytes 12670976 | tf_op jit(solution)/shard_map/add | solution.py:279
  416.3 103.8 %all-reduce.10.cloned.1.call-done = f32[137,32,512]{2,1,0:T(8,128)} async-done(((f32[137,32,512]{2,1,0:T(8,128)}), f32[137,32,512]{2,1,0:T(8,128)}) %all-reduce.10.cloned.1.call-update) | async-done | bytes 8978448 | tf_op jit(solution)/shard_map/psum | solution.py:298
  520.2 9.1 %concatenate.43 = f32[138,32,512]{2,1,0:T(8,128)} pad(f32[137,32,512]{2,1,0:T(8,128)} %all-reduce.10.cloned.1.call-done, f32[]{:T(128)} %constant.72.clone.1), padding=0_1x0_0x0_0 | pad | bytes 18022404 | tf_op jit(solution)/shard_map/concatenate | solution.py:299
  529.3 4.5 gather_fusion.1
  533.8 5.5 %multiply_subtract_fusion = (f32[27,32,512]{2,1,0:T(8,128)}, f32[27,32,512]{2,1,0:T(8,128)}, f32[27,32,512]{2,1,0:T(8,128)}) fusion(f32[27,32,512]{2,1,0:T(8,128)S(1)} %copy-done.12, f32[27,32,512]{2,1,0:T(8,128)S(1)} %gather_fusion.1, pred[27]{0:T(512)(128)(4,1)S(1)} %copy-done.68, f32[27,32,512]{2,1,0:T(8,128)} %param.13, f32[27,32,512]{2,1,0:T(8,128)} %param.14), kind=kLoop, calls=%fused_computation.127 | loop fusion | flops 7077888 | bytes 12386331 | tf_op jit(solution)/shard_map/sub | solution.py:306
  (252 shorter events, 93.3 us)
Async XLA Ops:
  7.2 115.2 %all-gather.2.cloned.1.call-start = ((), (), s32[]{:S(2)}) async-start(), calls=%async_computation | async-start | bytes 7962624 | tf_op jit(solution)/shard_map/all_gather | solution.py:120
  9.8 510.4 %all-reduce.10.cloned.1.call-start = ((), (), s32[]{:S(2)}) async-start(), calls=%async_computation.1 | async-start | bytes 17956864 | tf_op jit(solution)/shard_map/psum | solution.py:298
  10.6 41.3 %collective-permute-start = (bf16[2,3,512]{2,1,0:T(4,128)(2,1)S(1)}, bf16[2,3,512]{2,1,0:T(4,128)(2,1)S(1)}, u32[]{:S(2)}, u32[]{:S(2)}) collective-permute-start(bf16[2,3,512]{2,1,0:T(4,128)(2,1)S(1)} %get-tuple-element.55), channel_id=1, source_target_pairs={{0,1},{1,2},{2,3},{4,5},{5,6},{6,7},{8,9},{9,10},{10,11},{12,13},{... | collective-permute-start | bytes 18440 | tf_op jit(solution)/shard_map/ppermute | solution.py:36
  12.9 38.9 %collective-permute-start.1 = (bf16[2,3,512]{2,1,0:T(4,128)(2,1)S(1)}, bf16[2,3,512]{2,1,0:T(4,128)(2,1)S(1)}, u32[]{:S(2)}, u32[]{:S(2)}) collective-permute-start(bf16[2,3,512]{2,1,0:T(4,128)(2,1)S(1)} %get-tuple-element.54), channel_id=1, source_target_pairs={{1,0},{2,1},{3,2},{5,4},{6,5},{7,6},{9,8},{10,9},{11,10},{13,12},{... | collective-permute-start | bytes 18440 | tf_op jit(solution)/shard_map/ppermute | solution.py:39
  20.9 12.1 %copy-start.44 = (f32[320]{0:T(512)}, f32[320]{0:T(512)S(1)}, u32[]{:S(2)}) copy-start(f32[320]{0:T(512)S(1)} %get-tuple-element.75) | copy-start | bytes 3844
  20.9 12.1 %copy-start.46 = (f32[320]{0:T(512)}, f32[320]{0:T(512)S(1)}, u32[]{:S(2)}) copy-start(f32[320]{0:T(512)S(1)} %get-tuple-element.76) | copy-start | bytes 3844
  20.9 12.1 %copy-start.48 = (f32[320]{0:T(512)}, f32[320]{0:T(512)S(1)}, u32[]{:S(2)}) copy-start(f32[320]{0:T(512)S(1)} %get-tuple-element.77) | copy-start | bytes 3844
  20.9 12.1 %copy-start.50 = (f32[320]{0:T(512)}, f32[320]{0:T(512)S(1)}, u32[]{:S(2)}) copy-start(f32[320]{0:T(512)S(1)} %get-tuple-element.78) | copy-start | bytes 3844
  21.1 119.1 %copy-start.24 = (f32[2,1024]{1,0:T(2,128)}, f32[2,1024]{1,0:T(2,128)S(1)}, u32[]{:S(2)}) copy-start(f32[2,1024]{1,0:T(2,128)S(1)} %get-tuple-element.68) | copy-start | bytes 24580
  21.1 119.1 %copy-start.26 = (f32[2,1024]{1,0:T(2,128)}, f32[2,1024]{1,0:T(2,128)S(1)}, u32[]{:S(2)}) copy-start(f32[2,1024]{1,0:T(2,128)S(1)} %get-tuple-element.72) | copy-start | bytes 24580
  21.1 119.1 %copy-start.28 = (f32[2,1024]{1,0:T(2,128)}, f32[2,1024]{1,0:T(2,128)S(1)}, u32[]{:S(2)}) copy-start(f32[2,1024]{1,0:T(2,128)S(1)} %get-tuple-element.73) | copy-start | bytes 24580
  21.1 119.1 %copy-start.30 = (f32[2,1024]{1,0:T(2,128)}, f32[2,1024]{1,0:T(2,128)S(1)}, u32[]{:S(2)}) copy-start(f32[2,1024]{1,0:T(2,128)S(1)} %get-tuple-element.69) | copy-start | bytes 24580
  21.1 119.1 %copy-start.32 = (f32[2,1024]{1,0:T(2,128)}, f32[2,1024]{1,0:T(2,128)S(1)}, u32[]{:S(2)}) copy-start(f32[2,1024]{1,0:T(2,128)S(1)} %get-tuple-element.70) | copy-start | bytes 24580
  21.1 119.1 %copy-start.34 = (f32[2,1024]{1,0:T(2,128)}, f32[2,1024]{1,0:T(2,128)S(1)}, u32[]{:S(2)}) copy-start(f32[2,1024]{1,0:T(2,128)S(1)} %get-tuple-element.71) | copy-start | bytes 24580
  24.8 39.0 %collective-permute-start.3 = (f32[2,3,320]{1,2,0:T(8,128)}, f32[2,3,320]{1,2,0:T(8,128)}, u32[]{:S(2)}, u32[]{:S(2)}) collective-permute-start(f32[2,3,320]{1,2,0:T(8,128)} %slice.387), channel_id=1, source_target_pairs={{1,0},{2,1},{3,2},{5,4},{6,5},{7,6},{9,8},{10,9},{11,10},{13,12},{... | collective-permute-start | bytes 23048 | tf_op jit(solution)/shard_map/ppermute | solution.py:47
  51.8 105.1 %copy-start.36 = (s32[1,8,2,128]{3,1,2,0:T(8,128)}, s32[1,8,2,128]{3,1,2,0:T(8,128)S(1)}, u32[]{:S(2)}) copy-start(s32[1,8,2,128]{3,1,2,0:T(8,128)S(1)} %copy.53) | copy-start | bytes 24580
  137.4 14.7 %copy-start.13 = (bf16[4384,512]{1,0:T(8,128)(2,1)}, bf16[4384,512]{1,0:T(8,128)(2,1)S(1)}, u32[]{:S(2)}) copy-start(bf16[4384,512]{1,0:T(8,128)(2,1)S(1)} %bitcast_select_fusion) | copy-start | bytes 13467652
  140.1 8.7 %copy-start.53 = (f32[1,512]{1,0:T(1,128)}, f32[1,512]{1,0:T(1,128)S(1)}, u32[]{:S(2)}) copy-start(f32[1,512]{1,0:T(1,128)S(1)} %get-tuple-element.59) | copy-start | bytes 6148
  157.8 35.4 %copy-start.23 = (bf16[48,32,512]{2,1,0:T(8,128)(2,1)}, bf16[48,32,512]{2,1,0:T(8,128)(2,1)S(1)}, u32[]{:S(2)}) copy-start(bf16[48,32,512]{2,1,0:T(8,128)(2,1)S(1)} %get-tuple-element.45) | copy-start | bytes 4718596
  161.8 31.4 %copy-start.17 = (bf16[2048,512]{1,0:T(8,128)(2,1)}, bf16[2048,512]{1,0:T(8,128)(2,1)S(1)}, u32[]{:S(2)}) copy-start(bf16[2048,512]{1,0:T(8,128)(2,1)S(1)} %add_convert_fusion.3) | copy-start | bytes 6291460
  161.8 31.4 %copy-start.16 = (bf16[2,1024,512]{2,1,0:T(8,128)(2,1)S(1)}, bf16[2,1024,512]{2,1,0:T(8,128)(2,1)}, u32[]{:S(2)}) copy-start(bf16[2,1024,512]{2,1,0:T(8,128)(2,1)} %param.8) | copy-start | bytes 6291460
  253.1 16.6 %copy-start.4 = (f32[2048,512]{1,0:T(8,128)S(1)}, f32[2048,512]{1,0:T(8,128)}, u32[]{:S(2)}) copy-start(f32[2048,512]{1,0:T(8,128)} %bitcast_subtract_fusion) | copy-start | bytes 12582916
  253.1 16.6 %copy-start.6 = (f32[2048,512]{1,0:T(8,128)S(1)}, f32[2048,512]{1,0:T(8,128)}, u32[]{:S(2)}) copy-start(f32[2048,512]{1,0:T(8,128)} %fusion.60) | copy-start | bytes 12582916
  350.9 14.4 %copy-start.52 = (f32[4,320]{1,0:T(4,128)S(1)}, f32[4,320]{1,0:T(4,128)}, u32[]{:S(2)}) copy-start(f32[4,320]{1,0:T(4,128)} %multiply_subtract_fusion.2) | copy-start | bytes 15364
  376.4 10.4 %copy-start.45 = (f32[320]{0:T(512)S(1)}, f32[320]{0:T(512)}, u32[]{:S(2)}) copy-start(f32[320]{0:T(512)} %copy-done.44) | copy-start | bytes 3844
  376.4 10.4 %copy-start.47 = (f32[320]{0:T(512)S(1)}, f32[320]{0:T(512)}, u32[]{:S(2)}) copy-start(f32[320]{0:T(512)} %copy-done.46) | copy-start | bytes 3844
  376.4 10.4 %copy-start.49 = (f32[320]{0:T(512)S(1)}, f32[320]{0:T(512)}, u32[]{:S(2)}) copy-start(f32[320]{0:T(512)} %copy-done.48) | copy-start | bytes 3844
  376.4 10.4 %copy-start.51 = (f32[320]{0:T(512)S(1)}, f32[320]{0:T(512)}, u32[]{:S(2)}) copy-start(f32[320]{0:T(512)} %copy-done.50) | copy-start | bytes 3844
  376.4 10.3 %collective-permute-start.2 = (f32[2,3,320]{1,2,0:T(8,128)S(1)}, f32[2,3,320]{1,2,0:T(8,128)S(1)}, u32[]{:S(2)}, u32[]{:S(2)}) collective-permute-start(f32[2,3,320]{1,2,0:T(8,128)S(1)} %pad_add_fusion.1), channel_id=1, source_target_pairs={{0,1},{1,2},{2,3},{4,5},{5,6},{6,7},{8,9},{9,10},{10,11},{12,13},{... | collective-permute-start | bytes 23048 | tf_op jit(solution)/shard_map/ppermute | solution.py:47
  381.1 14.9 %collective-permute-start.4 = (f32[2,3,512]{2,1,0:T(4,128)S(1)}, f32[2,3,512]{2,1,0:T(4,128)S(1)}, u32[]{:S(2)}, u32[]{:S(2)}) collective-permute-start(f32[2,3,512]{2,1,0:T(4,128)S(1)} %get-tuple-element.49), channel_id=1, source_target_pairs={{1,0},{2,1},{3,2},{5,4},{6,5},{7,6},{9,8},{10,9},{11,10},{13,12},{... | collective-permute-start | bytes 36872 | tf_op jit(solution)/shard_map/ppermute | solution.py:39
  382.3 13.6 %collective-permute-start.5 = (f32[2,3,512]{2,1,0:T(4,128)S(1)}, f32[2,3,512]{2,1,0:T(4,128)S(1)}, u32[]{:S(2)}, u32[]{:S(2)}) collective-permute-start(f32[2,3,512]{2,1,0:T(4,128)S(1)} %get-tuple-element.50), channel_id=1, source_target_pairs={{0,1},{1,2},{2,3},{4,5},{5,6},{6,7},{8,9},{9,10},{10,11},{12,13},{... | collective-permute-start | bytes 36872 | tf_op jit(solution)/shard_map/ppermute | solution.py:36
  416.3 117.4 %copy-start.68 = (pred[27]{0:T(512)(128)(4,1)S(1)}, pred[27]{0:T(512)(128)(4,1)}, u32[]{:S(2)}) copy-start(pred[27]{0:T(512)(128)(4,1)} %get-tuple-element.18) | copy-start | bytes 85
  (54 other events, 251.3 us)
Sparse Core Ops, SparseCore 0:
  10.8 111.5 all-gather.1
  335.5 184.6 all-reduce.9
where the time goes:
time: 556 us; the launch traced here: 546 us
  other arithmetic  136 us (24%)
  local copies, waits for them, and re-layouts  133 us (24%)
  waiting for transfers between devices  130 us (23%)
  matrix products  119 us (21%)
  between operations  15.7 us (3%)
  starting transfers between devices  12.2 us (2%)
    dot_general x11, matrix products, contract(): lax.dot_general(left_side, right_side, (((left_dim,), (right_dim,)), ((),...  109 us
    psum x1, waiting for transfers between devices, local(): summed = lax.psum(grad_buckets, ('rows', 'seq'))  104 us
    another operation x3, other arithmetic  42.2 us
    concatenate x1, local copies, waits for them, and re-layouts, local(): jnp.concatenate([grad_w_in, grad_w_out, grad_w_head, vec_grads, in_rows,...  27.2 us
    all_gather x1, waiting for transfers between devices, local(): lax.all_gather(master.astype(jnp.bfloat16), 'rows', axis=0, tiled=True)  25.9 us
    add x1, other arithmetic, local(): input_grad + conv_weight[tap_index] * keep * halo_grad[:, begin:begin + f...  20.3 us
    unnamed x159, local copies, waits for them, and re-layouts  17.5 us
    reshape x1, local copies, waits for them, and re-layouts, local(): signal.reshape(rows_here, frames_here, lap_count, HOP)  14.4 us
  transfers between devices with their start and end apart: 8, of which 2 were waited for; matrix products, arithmetic and copies ran while one was open for 28% of the time, Pallas kernels for 0%

commit v1 on v0

--- a/solution.py
+++ b/solution.py
@@ -295,7 +295,7 @@
     )
     grad_buckets = jnp.pad(grad_table, ((0, NB * BR - PR), (0, 0))).reshape(NB, BR, channels)
     empty_bucket = jnp.zeros((1, BR, channels), jnp.float32)
-    summed = lax.psum(grad_buckets, ("rows", "seq"))
+    summed = jax.lax.psum(jax.lax.psum(grad_buckets, axis_name="seq"), axis_name="rows")
     extended = jnp.concatenate([summed, empty_bucket], axis=0)
     my_sources = lax.dynamic_slice_in_dim(source, lax.axis_index("rows") * slot_count, slot_count)
     reduced = jnp.take(extended, my_sources, axis=0)

time: 556 us -> 822 us (1.48)
  waiting for transfers between devices: 130 us -> 399 us
    psum x1 -> x2, waiting for transfers between devices: 104 us -> 372 us  [the longest x1 211 us: local(): jax.lax.psum(jax.lax.psum(grad_buckets, axis_name='seq'), axis_name='rows')]
  transfers between devices with their start and end apart: 8 -> 9, of which waited for: 2 -> 3; matrix products, arithmetic and copies ran while one was open for 28% -> 19% of each run, Pallas kernels for 0% -> 0%
where the time goes in v1:
time: 822 us; the launch traced here: 812 us
  waiting for transfers between devices  399 us (49%)
  other arithmetic  135 us (16%)
  local copies, waits for them, and re-layouts  133 us (16%)
  matrix products  119 us (14%)
  between operations  15.3 us (2%)
  starting transfers between devices  11.6 us (1%)
    psum x1, waiting for transfers between devices, local(): jax.lax.psum(jax.lax.psum(grad_buckets, axis_name='seq'), axis_name='rows')  211 us
    psum x1, waiting for transfers between devices, local(): jax.lax.psum(grad_buckets, axis_name='seq')  161 us
    dot_general x11, matrix products, contract(): lax.dot_general(left_side, right_side, (((left_dim,), (right_dim,)), ((),...  109 us
    another operation x3, other arithmetic  42.2 us
    all_gather x1, waiting for transfers between devices, local(): lax.all_gather(master.astype(jnp.bfloat16), 'rows', axis=0, tiled=True)  27.2 us
    concatenate x1, local copies, waits for them, and re-layouts, local(): jnp.concatenate([grad_w_in, grad_w_out, grad_w_head, vec_grads, in_rows,...  27.2 us
    add x1, other arithmetic, local(): input_grad + conv_weight[tap_index] * keep * halo_grad[:, begin:begin + f...  20.3 us
    unnamed x159, local copies, waits for them, and re-layouts  17.9 us
  transfers between devices with their start and end apart: 9, of which 3 were waited for; matrix products, arithmetic and copies ran while one was open for 19% of the time, Pallas kernels for 0%

profile of v1, /device:TPU:0, one launch (start us, length us, event | category | flops | bytes accessed | tf_op | source)
XLA Modules:
  0.0 812.4 jit_solution(517489518048528327)
XLA Ops:
  34.9 15.2 %multiply_convert_fusion.2 = (bf16[641,1280]{1,0:T(8,128)(2,1)}, bf16[641,1280]{1,0:T(8,128)(2,1)}) fusion(f32[641]{0:T(1024)S(1)} %fusion.74, f32[641]{0:T(1024)S(1)} %select_multiply_fusion), kind=kLoop, calls=%fused_computation.89 | loop fusion | flops 10666240 | bytes 3287048 | tf_op jit(solution)/shard_map/convert.12
  50.4 9.4 %concatenate.35 = bf16[2,1030,512]{2,1,0:T(8,128)(2,1)S(1)} concatenate(bf16[2,3,512]{2,1,0:T(4,128)(2,1)S(1)} %collective-permute-done, bf16[2,1024,512]{2,1,0:T(8,128)(2,1)} %param.8, bf16[2,3,512]{2,1,0:T(4,128)(2,1)S(1)} %collective-permute-done.1), dimensions={1} | concatenate | bytes 4218880 | tf_op jit(solution)/shard_map/concatenate | solution.py:40
  62.5 4.6 fusion.55
  70.3 10.2 %copy.40 = bf16[2,1024,4,320]{1,0,3,2:T(2,128)(2,1)} copy(bf16[2,1024,4,320]{1,3,0,2:T(8,128)(2,1)} %pad_maximum_fusion.1) | data formatting | bytes 10485760 | tf_op jit(solution)/shard_map/stack | solution.py:216
  80.5 4.9 copy.45
  85.4 9.7 %fusion.49 = f32[2048,1282]{0,1:T(8,128)} fusion(bf16[2048,1280]{0,1:T(8,128)(2,1)S(1)} %bitcast.122, bf16[641,1280]{1,0:T(8,128)(2,1)S(1)} %copy-done.20, bf16[641,1280]{1,0:T(8,128)(2,1)S(1)} %copy-done.21), kind=kOutput, calls=%fused_computation.122 | convolution fusion | flops 6727936000 | bytes 19026944 | tf_op jit(solution)/shard_map/dot_general | solution.py:104
  95.1 27.2 %all-gather.2.cloned.1.call-done = bf16[216,32,512]{2,1,0:T(8,128)(2,1)} async-done(((bf16[27,32,512]{2,1,0:T(8,128)(2,1)}), bf16[216,32,512]{2,1,0:T(8,128)(2,1)}) %all-gather.2.cloned.1.call-update) | async-done | bytes 7077904 | tf_op jit(solution)/shard_map/all_gather | solution.py:120
  122.3 10.9 %gather_fusion = bf16[137,32,512]{2,1,0:T(8,128)(2,1)} fusion(bf16[216,32,512]{2,1,0:T(8,128)(2,1)} %all-gather.2.cloned.1.call-done, s32[1024]{0:T(1024)S(1)} %pad_clamp_fusion.1), kind=kCustom, calls=%fused_computation | custom fusion | bytes 8978980 | tf_op jit(solution)/shard_map/jit(_take)/gather | solution.py:121
  133.3 4.1 bitcast_select_fusion
  142.7 6.1 fusion.88
  161.8 31.4 %multiply_convert_fusion = (bf16[2048,1536]{1,0:T(8,128)(2,1)S(1)}, f32[2048,1536]{1,0:T(8,128)}, f32[2048,1536]{1,0:T(8,128)}) fusion(f32[1536]{0:T(1024)S(1)} %reshape.280, bf16[2048,512]{1,0:T(8,128)(2,1)S(1)} %add_convert_fusion.3, bf16[1536,512]{1,0:T(8,128)(2,1)S(1)} %bitcast.123), kind=kOutput, calls=%fused_computation.6 | convolution fusion | flops 3428843520 | bytes 35133440 | tf_op jit(solution)/shard_map/dot_general | solution.py:104
  193.2 5.6 fusion.86
  201.6 5.8 convolution_add_fusion
  207.5 24.2 %add_convert_fusion.1 = (bf16[2048,641]{0,1:T(8,128)(2,1)S(1)}, bf16[2048,641]{0,1:T(8,128)(2,1)S(1)}, bf16[2048,641]{0,1:T(8,128)(2,1)}, bf16[2048,641]{0,1:T(8,128)(2,1)}) fusion(f32[2048,1282]{0,1:T(8,128)} %fusion.49, f32[2048,1282]{0,1:T(8,128)S(1)} %convolution_add_fusion), kind=kLoop, calls=%fused_computation.31 | loop fusion | flops 15753216 | bytes 31506432 | tf_op jit(solution)/shard_map/convert.2
  233.8 6.2 multiply_reduce_fusion
  240.0 4.6 fusion.52
  253.1 16.6 %convert_reduce_fusion = (f32[1536]{0:T(1024)S(1)}, bf16[2048,1536]{1,0:T(8,128)(2,1)}) fusion(f32[2048,1536]{1,0:T(8,128)} %get-tuple-element.33, bf16[2048,512]{1,0:T(8,128)(2,1)} %copy-done.19, bf16[1536,512]{1,0:T(8,128)(2,1)} %bitcast.126, f32[2048,1536]{1,0:T(8,128)} %get-tuple-element.84, f32[1536]{0:T(1024)S(1)} %reshape.280), kind=kOutput, calls=%fused_computation.4 | convolution fusion | flops 3274701312 | bytes 35139584 | tf_op jit(solution)/shard_map/dot_general | solution.py:104
  269.7 6.7 multiply_reduce_fusion.9
  276.4 5.1 fusion.94
  285.4 5.5 fusion.84
  294.7 5.3 multiply_reduce_fusion.2
  300.0 27.2 %concatenate.42 = f32[4380,512]{1,0:T(8,128)} concatenate(f32[1536,512]{1,0:T(8,128)} %fusion.94, f32[1536,512]{1,0:T(8,128)S(1)} %fusion.95, f32[1282,512]{1,0:T(8,128)} %fusion.52, f32[1,512]{1,0:T(1,128)S(1)} %bitcast.156, f32[1,512]{1,0:T(1,128)S(1)} %bitcast.155, f32[1,512]{1,0:T(1,128)S(1)} %bitcast.154, f32[1,512]{1,0:T(1,128)S(1)} %bitcast.153, f32[1,512]{1,0:T(1,128)S(1)} %bitcast.152, ...), dimensions={0} | concatenate | bytes 17940480 | tf_op jit(solution)/shard_map/concatenate | solution.py:293
  327.2 8.1 pad.35
  335.4 160.7 %all-reduce.11.cloned.1.call-done = f32[137,32,512]{2,1,0:T(8,128)} async-done(((f32[137,32,512]{2,1,0:T(8,128)}), f32[137,32,512]{2,1,0:T(8,128)}) %all-reduce.11.cloned.1.call-update) | async-done | bytes 8978448 | tf_op jit(solution)/shard_map/psum | solution.py:298
  497.9 13.5 %fusion.6 = f32[2048,1280]{0,1:T(8,128)} fusion(bf16[2048,641]{0,1:T(8,128)(2,1)} %get-tuple-element.41, bf16[2048,641]{0,1:T(8,128)(2,1)S(1)} %copy-done.15, bf16[641,1280]{1,0:T(8,128)(2,1)} %get-tuple-element.91, bf16[641,1280]{1,0:T(8,128)(2,1)} %get-tuple-element.92), kind=kOutput, calls=%fused_computation.34 | convolution fusion | flops 6738438144 | bytes 19018752 | tf_op jit(solution)/shard_map/dot_general | solution.py:104
  511.4 14.3 %reshape.268 = f32[2,1024,4,320]{1,0,3,2:T(2,128)} reshape(f32[2048,1280]{0,1:T(8,128)} %fusion.6) | data formatting | bytes 20971520 | tf_op jit(solution)/shard_map/reshape | solution.py:189
  525.7 8.5 %copy_multiply_fusion = f32[2,1024,4,320]{1,3,0,2:T(8,128)S(1)} fusion(f32[2,1024,4,320]{1,0,3,2:T(2,128)} %reshape.268, f32[4,320]{1,0:T(4,128)S(1)} %multiply_subtract_fusion.2), kind=kLoop, calls=%fused_computation.21 | loop fusion | flops 2621440 | bytes 20976640 | tf_op jit(solution)/shard_map/mul | solution.py:189
  555.3 20.3 %fusion.13 = f32[2,1024,512]{2,1,0:T(8,128)} fusion(f32[2,3,512]{2,1,0:T(4,128)S(1)} %collective-permute-done.5, f32[2,3,512]{2,1,0:T(4,128)S(1)} %collective-permute-done.4, f32[2,1024,512]{2,1,0:T(8,128)} %bitcast.119, f32[2,1024,512]{2,1,0:T(8,128)} %bitcast.118, f32[512]{0:T(512)S(1)} %bitcast.135, f32[2,1024]{1,0:T(2,128)S(1)} %copy-done.31, ...), kind=kLoop, calls=%fused_computation.46 | loop fusion | flops 27262976 | bytes 12670976 | tf_op jit(solution)/shard_map/add | solution.py:279
  575.6 211.1 %all-reduce.13.cloned.1.call-done = f32[137,32,512]{2,1,0:T(8,128)} async-done(((f32[137,32,512]{2,1,0:T(8,128)}), f32[137,32,512]{2,1,0:T(8,128)}) %all-reduce.13.cloned.1.call-update) | async-done | bytes 8978448 | tf_op jit(solution)/shard_map/psum | solution.py:298
  786.7 9.1 %concatenate.43 = f32[138,32,512]{2,1,0:T(8,128)} pad(f32[137,32,512]{2,1,0:T(8,128)} %all-reduce.13.cloned.1.call-done, f32[]{:T(128)} %constant.72.clone.1), padding=0_1x0_0x0_0 | pad | bytes 18022404 | tf_op jit(solution)/shard_map/concatenate | solution.py:299
  795.8 4.4 gather_fusion.1
  800.2 5.5 multiply_subtract_fusion
  (255 shorter events, 95.3 us)
Async XLA Ops:
  7.2 115.1 %all-gather.2.cloned.1.call-start = ((), (), s32[]{:S(2)}) async-start(), calls=%async_computation | async-start | bytes 7962624 | tf_op jit(solution)/shard_map/all_gather | solution.py:120
  9.8 486.3 %all-reduce.11.cloned.1.call-start = ((), (), s32[]{:S(2)}) async-start(), calls=%async_computation.1 | async-start | bytes 17956864 | tf_op jit(solution)/shard_map/psum | solution.py:298
  10.6 39.8 %collective-permute-start = (bf16[2,3,512]{2,1,0:T(4,128)(2,1)S(1)}, bf16[2,3,512]{2,1,0:T(4,128)(2,1)S(1)}, u32[]{:S(2)}, u32[]{:S(2)}) collective-permute-start(bf16[2,3,512]{2,1,0:T(4,128)(2,1)S(1)} %get-tuple-element.55), channel_id=1, source_target_pairs={{0,1},{1,2},{2,3},{4,5},{5,6},{6,7},{8,9},{9,10},{10,11},{12,13},{... | collective-permute-start | bytes 18440 | tf_op jit(solution)/shard_map/ppermute | solution.py:36
  12.9 37.4 %collective-permute-start.1 = (bf16[2,3,512]{2,1,0:T(4,128)(2,1)S(1)}, bf16[2,3,512]{2,1,0:T(4,128)(2,1)S(1)}, u32[]{:S(2)}, u32[]{:S(2)}) collective-permute-start(bf16[2,3,512]{2,1,0:T(4,128)(2,1)S(1)} %get-tuple-element.54), channel_id=1, source_target_pairs={{1,0},{2,1},{3,2},{5,4},{6,5},{7,6},{9,8},{10,9},{11,10},{13,12},{... | collective-permute-start | bytes 18440 | tf_op jit(solution)/shard_map/ppermute | solution.py:39
  20.9 11.2 %copy-start.44 = (f32[320]{0:T(512)}, f32[320]{0:T(512)S(1)}, u32[]{:S(2)}) copy-start(f32[320]{0:T(512)S(1)} %get-tuple-element.75) | copy-start | bytes 3844
  20.9 11.2 %copy-start.46 = (f32[320]{0:T(512)}, f32[320]{0:T(512)S(1)}, u32[]{:S(2)}) copy-start(f32[320]{0:T(512)S(1)} %get-tuple-element.76) | copy-start | bytes 3844
  20.9 11.2 %copy-start.48 = (f32[320]{0:T(512)}, f32[320]{0:T(512)S(1)}, u32[]{:S(2)}) copy-start(f32[320]{0:T(512)S(1)} %get-tuple-element.77) | copy-start | bytes 3844
  20.9 11.2 %copy-start.50 = (f32[320]{0:T(512)}, f32[320]{0:T(512)S(1)}, u32[]{:S(2)}) copy-start(f32[320]{0:T(512)S(1)} %get-tuple-element.78) | copy-start | bytes 3844
  21.1 119.1 %copy-start.24 = (f32[2,1024]{1,0:T(2,128)}, f32[2,1024]{1,0:T(2,128)S(1)}, u32[]{:S(2)}) copy-start(f32[2,1024]{1,0:T(2,128)S(1)} %get-tuple-element.68) | copy-start | bytes 24580
  21.1 119.1 %copy-start.26 = (f32[2,1024]{1,0:T(2,128)}, f32[2,1024]{1,0:T(2,128)S(1)}, u32[]{:S(2)}) copy-start(f32[2,1024]{1,0:T(2,128)S(1)} %get-tuple-element.72) | copy-start | bytes 24580
  21.1 119.1 %copy-start.28 = (f32[2,1024]{1,0:T(2,128)}, f32[2,1024]{1,0:T(2,128)S(1)}, u32[]{:S(2)}) copy-start(f32[2,1024]{1,0:T(2,128)S(1)} %get-tuple-element.73) | copy-start | bytes 24580
  21.1 119.1 %copy-start.30 = (f32[2,1024]{1,0:T(2,128)}, f32[2,1024]{1,0:T(2,128)S(1)}, u32[]{:S(2)}) copy-start(f32[2,1024]{1,0:T(2,128)S(1)} %get-tuple-element.69) | copy-start | bytes 24580
  21.1 119.1 %copy-start.32 = (f32[2,1024]{1,0:T(2,128)}, f32[2,1024]{1,0:T(2,128)S(1)}, u32[]{:S(2)}) copy-start(f32[2,1024]{1,0:T(2,128)S(1)} %get-tuple-element.70) | copy-start | bytes 24580
  21.1 119.1 %copy-start.34 = (f32[2,1024]{1,0:T(2,128)}, f32[2,1024]{1,0:T(2,128)S(1)}, u32[]{:S(2)}) copy-start(f32[2,1024]{1,0:T(2,128)S(1)} %get-tuple-element.71) | copy-start | bytes 24580
  24.8 37.5 %collective-permute-start.3 = (f32[2,3,320]{1,2,0:T(8,128)}, f32[2,3,320]{1,2,0:T(8,128)}, u32[]{:S(2)}, u32[]{:S(2)}) collective-permute-start(f32[2,3,320]{1,2,0:T(8,128)} %slice.387), channel_id=1, source_target_pairs={{1,0},{2,1},{3,2},{5,4},{6,5},{7,6},{9,8},{10,9},{11,10},{13,12},{... | collective-permute-start | bytes 23048 | tf_op jit(solution)/shard_map/ppermute | solution.py:47
  50.3 106.6 %copy-start.36 = (s32[1,8,2,128]{3,1,2,0:T(8,128)}, s32[1,8,2,128]{3,1,2,0:T(8,128)S(1)}, u32[]{:S(2)}) copy-start(s32[1,8,2,128]{3,1,2,0:T(8,128)S(1)} %copy.53) | copy-start | bytes 24580
  137.4 14.7 %copy-start.13 = (bf16[4384,512]{1,0:T(8,128)(2,1)}, bf16[4384,512]{1,0:T(8,128)(2,1)S(1)}, u32[]{:S(2)}) copy-start(bf16[4384,512]{1,0:T(8,128)(2,1)S(1)} %bitcast_select_fusion) | copy-start | bytes 13467652
  140.1 8.7 %copy-start.52 = (f32[1,512]{1,0:T(1,128)}, f32[1,512]{1,0:T(1,128)S(1)}, u32[]{:S(2)}) copy-start(f32[1,512]{1,0:T(1,128)S(1)} %get-tuple-element.59) | copy-start | bytes 6148
  140.1 8.7 %copy-start.54 = (f32[1,512]{1,0:T(1,128)}, f32[1,512]{1,0:T(1,128)S(1)}, u32[]{:S(2)}) copy-start(f32[1,512]{1,0:T(1,128)S(1)} %get-tuple-element.60) | copy-start | bytes 6148
  157.8 35.4 %copy-start.23 = (bf16[48,32,512]{2,1,0:T(8,128)(2,1)}, bf16[48,32,512]{2,1,0:T(8,128)(2,1)S(1)}, u32[]{:S(2)}) copy-start(bf16[48,32,512]{2,1,0:T(8,128)(2,1)S(1)} %get-tuple-element.45) | copy-start | bytes 4718596
  161.8 31.4 %copy-start.17 = (bf16[2048,512]{1,0:T(8,128)(2,1)}, bf16[2048,512]{1,0:T(8,128)(2,1)S(1)}, u32[]{:S(2)}) copy-start(bf16[2048,512]{1,0:T(8,128)(2,1)S(1)} %add_convert_fusion.3) | copy-start | bytes 6291460
  161.8 31.4 %copy-start.16 = (bf16[2,1024,512]{2,1,0:T(8,128)(2,1)S(1)}, bf16[2,1024,512]{2,1,0:T(8,128)(2,1)}, u32[]{:S(2)}) copy-start(bf16[2,1024,512]{2,1,0:T(8,128)(2,1)} %param.8) | copy-start | bytes 6291460
  253.1 16.6 %copy-start.4 = (f32[2048,512]{1,0:T(8,128)S(1)}, f32[2048,512]{1,0:T(8,128)}, u32[]{:S(2)}) copy-start(f32[2048,512]{1,0:T(8,128)} %bitcast_subtract_fusion) | copy-start | bytes 12582916
  253.1 16.6 %copy-start.6 = (f32[2048,512]{1,0:T(8,128)S(1)}, f32[2048,512]{1,0:T(8,128)}, u32[]{:S(2)}) copy-start(f32[2048,512]{1,0:T(8,128)} %fusion.60) | copy-start | bytes 12582916
  335.3 451.3 %all-reduce.13.cloned.1.call-start = ((), (), s32[]{:S(2)}) async-start(), calls=%async_computation.2 | async-start | bytes 17956864 | tf_op jit(solution)/shard_map/psum | solution.py:298
  536.7 9.7 %copy-start.45 = (f32[320]{0:T(512)S(1)}, f32[320]{0:T(512)}, u32[]{:S(2)}) copy-start(f32[320]{0:T(512)} %copy-done.44) | copy-start | bytes 3844
  536.7 9.7 %copy-start.47 = (f32[320]{0:T(512)S(1)}, f32[320]{0:T(512)}, u32[]{:S(2)}) copy-start(f32[320]{0:T(512)} %copy-done.46) | copy-start | bytes 3844
  536.7 9.7 %copy-start.49 = (f32[320]{0:T(512)S(1)}, f32[320]{0:T(512)}, u32[]{:S(2)}) copy-start(f32[320]{0:T(512)} %copy-done.48) | copy-start | bytes 3844
  536.7 9.7 %copy-start.51 = (f32[320]{0:T(512)S(1)}, f32[320]{0:T(512)}, u32[]{:S(2)}) copy-start(f32[320]{0:T(512)} %copy-done.50) | copy-start | bytes 3844
  536.7 9.7 %collective-permute-start.2 = (f32[2,3,320]{1,2,0:T(8,128)S(1)}, f32[2,3,320]{1,2,0:T(8,128)S(1)}, u32[]{:S(2)}, u32[]{:S(2)}) collective-permute-start(f32[2,3,320]{1,2,0:T(8,128)S(1)} %pad_add_fusion.1), channel_id=1, source_target_pairs={{0,1},{1,2},{2,3},{4,5},{5,6},{6,7},{8,9},{9,10},{10,11},{12,13},{... | collective-permute-start | bytes 23048 | tf_op jit(solution)/shard_map/ppermute | solution.py:47
  541.6 13.6 %collective-permute-start.4 = (f32[2,3,512]{2,1,0:T(4,128)S(1)}, f32[2,3,512]{2,1,0:T(4,128)S(1)}, u32[]{:S(2)}, u32[]{:S(2)}) collective-permute-start(f32[2,3,512]{2,1,0:T(4,128)S(1)} %get-tuple-element.49), channel_id=1, source_target_pairs={{1,0},{2,1},{3,2},{5,4},{6,5},{7,6},{9,8},{10,9},{11,10},{13,12},{... | collective-permute-start | bytes 36872 | tf_op jit(solution)/shard_map/ppermute | solution.py:39
  542.9 12.3 %collective-permute-start.5 = (f32[2,3,512]{2,1,0:T(4,128)S(1)}, f32[2,3,512]{2,1,0:T(4,128)S(1)}, u32[]{:S(2)}, u32[]{:S(2)}) collective-permute-start(f32[2,3,512]{2,1,0:T(4,128)S(1)} %get-tuple-element.50), channel_id=1, source_target_pairs={{0,1},{1,2},{2,3},{4,5},{5,6},{6,7},{8,9},{9,10},{10,11},{12,13},{... | collective-permute-start | bytes 36872 | tf_op jit(solution)/shard_map/ppermute | solution.py:36
  (55 other events, 242.5 us)
Sparse Core Ops, SparseCore 0:
  10.8 111.4 all-gather.1
  335.5 160.5 all-reduce.10
  500.0 286.6 all-reduce.12
